TPU v7x, 32 devices: a whole 2x2x4 slice. The times are simulated.
32 devices in a mesh: rows: 8 (over z, y), heads: 4 (over x, core).
Axes of the slice: x: 2, y: 2, z: 4, core: 2. Of those that a mesh axis runs over, the one named last changes fastest.
Arguments:
- tokens: bfloat16 [24576, 768], P(('rows', 'heads')), may hold values from -6 to 6
- lengths: int32 [24, 24], P('rows'), may hold values from 1 to 512, 1024 in all within a row
- w_query: bfloat16 [768, 768], P(None, 'heads'), may hold values from -0.21875 to 0.21875
- w_key: bfloat16 [768, 768], P(None, 'heads'), may hold values from -0.21875 to 0.21875
- w_value: bfloat16 [768, 768], P(None, 'heads'), may hold values from -0.21875 to 0.21875
- w_out: bfloat16 [768, 768], P('heads'), may hold values from -0.625 to 0.625
- w_up: bfloat16 [768, 3072], P(None, 'heads'), may hold values from -0.21875 to 0.21875
- w_down: bfloat16 [3072, 768], P('heads'), may hold values from -0.109375 to 0.109375
- gain_first: bfloat16 [768], P('heads'), may hold values from 0.5 to 1.5
- shift_first: bfloat16 [768], P('heads'), may hold values from -3 to 3
- gain_second: bfloat16 [768], P('heads'), may hold values from 0.5 to 1.5
- shift_second: bfloat16 [768], P('heads'), may hold values from -3 to 3
- cotangent: bfloat16 [24576, 768], P(('rows', 'heads')), may hold values from -6 to 6
Outputs:
- mixed: bfloat16 [24576, 768], P(('rows', 'heads'))
- grad_tokens: float32 [24576, 768], P(('rows', 'heads'))
- grad_query: float32 [768, 768], P(None, 'heads')
- grad_key: float32 [768, 768], P(None, 'heads')
- grad_value: float32 [768, 768], P(None, 'heads')
- grad_out: float32 [768, 768], P('heads')
- grad_up: float32 [768, 3072], P(None, 'heads')
- grad_down: float32 [3072, 768], P('heads')
- grad_gain_first: float32 [768], P('heads')
- grad_shift_first: float32 [768], P('heads')
- grad_gain_second: float32 [768], P('heads')
- grad_shift_second: float32 [768], P('heads')
Inputs may be any that keep to these rules, and one draw needn't show every extreme that they name: `lengths`: each packed row of 1024 tokens is filled exactly by its 24 documents, and every row holds one document of exactly 512 tokens.
All inputs are finite; a program needn't handle non-finite values.
Results may differ from a plain program's by a relative error of at most 0.013.
Values may be sent and summed in bfloat16 or wider, within the bound.
A program may use at most 128 MiB of HBM per device.

v0:
```python
import functools

import jax
import jax.numpy as jnp
from jax import lax
from jax.experimental import pallas as pl
from jax.experimental.pallas import tpu as pltpu
from jax.sharding import PartitionSpec as P

MESH = pl.DeviceIdType.MESH
BF = jnp.bfloat16
F32 = jnp.float32
HEAD_WIDTH = 64
LONGEST_DOC = 512
BLK = 256
HALO = LONGEST_DOC // BLK
NORM_EPS = 1e-12
VMEM_LIMIT = 62 * 1024 * 1024


def nt(left, right):
    return lax.dot_general(left, right, (((1,), (1,)), ((), ())), preferred_element_type=F32)


def nn(left, right):
    return lax.dot_general(left, right, (((1,), (0,)), ((), ())), preferred_element_type=F32)


def flip(index, bit):
    return index + bit - 2 * bit * ((index // bit) % 2)


def place():
    r, h = lax.axis_index("rows"), lax.axis_index("heads")
    return r, h


def greet(ids):
    barrier = pltpu.get_barrier_semaphore()
    for who in ids:
        pl.semaphore_signal(barrier, inc=1, device_id=who, device_id_type=MESH)
    pl.semaphore_wait(barrier, len(ids))


def group_of(r, h, groups):
    return [(r, lax.rem(h + i, groups)) for i in range(1, groups)]


def remote(src, dst, send, recv, who):
    return pltpu.make_async_remote_copy(
        src_ref=src, dst_ref=dst, send_sem=send, recv_sem=recv, device_id=who, device_id_type=MESH
    )


class Gather:
    def __init__(self, own, full, sems, at):
        self.own, self.full, self.sems, self.at = own, full, sems, at
        self.n = own.shape[1]
        self.u = self.n // 12
        r, h = place()
        self.r, self.h = r, h
        y, z = r % 2, (r // 2) % 2
        self.k = 2 * z + y
        self.ky = 2 * z + 1 - y
        self.kz = 2 * (1 - z) + y
        self.kd = 3 - self.k
        self.hx = flip(h, 2)
        self.hc = flip(h, 1)
        self.by_x = (r, self.hx)
        self.by_c = (r, self.hc)
        self.by_y = (flip(r, 1), h)
        self.by_z = (flip(r, 2), h)

    def rows(self, shard, sub, count):
        u = self.u
        return pl.ds(pl.multiple_of(shard * self.n + sub * u, 16), count * u)

    def part(self, slot, who, shard, sub, count, own=False):
        dst = self.full.at[:, self.rows(shard, sub, count), :]
        src = self.own.at[:, self.rows(0, sub, count), :] if own else dst
        send, recv = self.sems
        return remote(src, dst, send.at[self.at, slot], recv.at[self.at, slot], who)

    def x_main(self):
        return self.part(0, self.by_x, self.h, 3 * self.k, 3, own=True)

    def x_diag(self):
        return self.part(1, self.by_x, self.h, 3 * self.kd, 1, own=True)

    def y_main(self):
        return self.part(2, self.by_y, self.hx, 3 * self.k, 3)

    def z_main(self):
        return self.part(3, self.by_z, self.hx, 3 * self.k, 3)

    def y_diag(self):
        return self.part(4, self.by_y, self.hx, 3 * self.kz + 1, 1)

    def z_diag(self):
        return self.part(5, self.by_z, self.hx, 3 * self.ky + 2, 1)

    def c_own(self):
        return self.part(6, self.by_c, self.h, 0, 12, own=True)

    def c_part(self, i):
        return self.part(7 + i, self.by_c, self.hx, 3 * (self.k, self.ky, self.kz, self.kd)[i], 3)

    def local(self):
        send, _ = self.sems
        return pltpu.make_async_copy(
            self.own, self.full.at[:, self.rows(self.h, 0, 12), :], send.at[self.at, 11]
        )

    def start_x(self):
        self.x_main().start()
        self.x_diag().start()

    def start_main(self):
        self.x_main().start()

    def start_diag(self):
        self.x_diag().start()

    def start_c(self, keep):
        self.c_own().start()
        if keep:
            self.local().start()

    def step_x(self):
        self.x_main().wait_recv()
        self.y_main().start()
        self.z_main().start()
        self.c_part(0).start()

    def step_yz(self):
        self.y_main().wait_recv()
        self.z_diag().start()
        self.c_part(1).start()
        self.z_main().wait_recv()
        self.y_diag().start()
        self.c_part(2).start()

    def step_diag(self):
        self.x_diag().wait_recv()
        self.y_diag().wait_recv()
        self.z_diag().wait_recv()
        self.c_part(3).start()

    def near(self, keep):
        self.c_own().wait_recv()
        if keep:
            self.local().wait()

    def far(self):
        for i in range(4):
            self.c_part(i).wait_recv()

    def sent(self):
        for copy in (self.x_main(), self.x_diag(), self.y_main(), self.z_main(), self.y_diag(), self.z_diag(), self.c_own()):
            copy.wait_send()
        for i in range(4):
            self.c_part(i).wait_send()


def window_start(h, j, own_blocks, row_blocks):
    g = own_blocks * h + j
    first = own_blocks * h - HALO
    row = row_blocks * (g // row_blocks)
    return jnp.clip(row, first, first + own_blocks + 2 * HALO - row_blocks) - first


def mask_of(keys, queries):
    down = jnp.broadcast_to(keys, (8, BLK)).T[:, 0:1]
    return jnp.where(down == queries, 0.0, -1e30).astype(F32)


ANY = pl.BlockSpec(memory_space=pl.ANY)
VM = pl.BlockSpec(memory_space=pltpu.VMEM)


def gelu_parts(u):
    bell = jnp.exp(-0.5 * u * u)
    base = 1.0 + (0.3275911 * 0.7071067811865476) * jnp.abs(u)
    t = pl.reciprocal(base, approx=True)
    t = t * (2.0 - base * t)
    poly = t * (0.127414796 + t * (-0.142248368 + t * (0.7107068705 + t * (-0.7265760135 + t * 0.5307027145))))
    tail = poly * bell
    cdf = jnp.where(u >= 0.0, 1.0 - tail, tail)
    return u * cdf, cdf + u * (bell * 0.3989422804014327)


class Sum:
    def __init__(self, n, bits, bufs, sems, at, turned):
        self.n, self.bits, self.at = n, bits, at
        self.mine, self.rc, self.rx, self.ry, self.rz, self.rest = bufs
        self.send, self.recv, self.keep = sems
        r, h = place()
        self.y, self.z = r % 2, (r // 2) % 2
        self.by_x, self.by_c = (r, flip(h, 2)), (r, flip(h, 1))
        self.by_y, self.by_z = (flip(r, 1), h), (flip(r, 2), h)
        if turned:
            self.y, self.z, self.by_y, self.by_z = self.z, self.y, self.by_z, self.by_y
        self.by_rest = [(flip(r, b), h) for b in bits]

    def copy(self, slot, src, dst, who):
        return remote(src, dst, self.send.at[self.at, slot], self.recv.at[self.at, slot], who)

    def core(self, i):
        return self.copy(i, self.mine.at[0], self.rc.at[i], self.by_c)

    def x(self):
        return self.copy(2, self.mine.at[1], self.rx, self.by_x)

    def half(self, which):
        return pl.ds(pl.multiple_of(which * (self.n // 2), 16), self.n // 2)

    def quarter(self, half, which):
        return pl.ds(pl.multiple_of(half * (self.n // 2) + which * (self.n // 4), 16), self.n // 4)

    def own(self):
        return self.mine.at[2, self.quarter(self.y, self.z), :]

    def landed(self, half, which):
        return self.rx.at[self.quarter(half, which), :]

    def y_down(self):
        return self.copy(3, self.mine.at[2, self.half(1 - self.y), :], self.ry, self.by_y)

    def z_down(self):
        return self.copy(4, self.mine.at[2, self.quarter(self.y, 1 - self.z), :], self.rz, self.by_z)

    def z_up(self):
        return self.copy(5, self.own(), self.landed(self.y, self.z), self.by_z)

    def y_up(self):
        return self.copy(6, self.own(), self.landed(self.y, self.z), self.by_y)

    def y_up2(self):
        return self.copy(7, self.landed(self.y, 1 - self.z), self.landed(self.y, 1 - self.z), self.by_y)

    def swap(self, i):
        return self.copy(8 + i, self.own(), self.rest.at[i], self.by_rest[i])

    def add(self, ref, got):
        step = self.n // 4

        def some(i, c):
            at = pl.ds(pl.multiple_of(i * step, 16), step)
            ref[at, :] = (ref[at, :].astype(F32) + got[at, :].astype(F32)).astype(BF)
            return c

        lax.fori_loop(0, ref.shape[0] // step, some, 0)

    def c0(self):
        self.core(0).start()

    def f(self):
        self.core(0).wait_recv()
        self.add(self.mine.at[1], self.rc.at[0])

    def xs(self):
        self.x().start()

    def c1(self):
        self.core(1).start()

    def s(self):
        self.core(1).wait_recv()
        self.add(self.mine.at[2], self.rc.at[1])

    def r(self):
        self.x().wait_recv()
        self.add(self.mine.at[2], self.rx)
        self.y_down().start()

    def yy(self):
        self.y_down().wait_recv()
        self.add(self.mine.at[2, self.half(self.y), :], self.ry)
        self.z_down().start()

    def zz(self):
        self.z_down().wait_recv()
        self.add(self.own(), self.rz)
        if self.bits:
            self.swap(0).start()

    def w(self):
        for i in range(len(self.bits)):
            self.swap(i).wait_recv()
            self.swap(i).wait_send()
            self.add(self.own(), self.rest.at[i])
            if i + 1 < len(self.bits):
                self.swap(i + 1).start()
        self.z_up().start()
        self.y_up().start()

    def u(self):
        self.z_up().wait_recv()
        self.y_up2().start()

    def outs(self, out, lo):
        def local(i, src, rows):
            start = pl.multiple_of(lo + rows.start, 16)
            return pltpu.make_async_copy(src, out.at[pl.ds(start, rows.size), :], self.keep.at[self.at, i])

        mine, beside, other = self.quarter(self.y, self.z), self.quarter(self.y, 1 - self.z), self.half(1 - self.y)
        return (
            local(0, self.own(), mine),
            local(1, self.rx.at[beside, :], beside),
            local(2, self.rx.at[other, :], other),
        )

    def e(self, out, lo):
        self.y_up().wait_recv()
        self.y_up2().wait_recv()
        for c in self.outs(out, lo):
            c.start()

    def sent(self, out, lo):
        for c in (self.core(1), self.x(), self.y_down(), self.z_down(), self.z_up(), self.y_up(), self.y_up2()):
            c.wait_send()
        for c in self.outs(out, lo):
            c.wait()


def other_bits(count):
    bits, b = [], 4
    while b < count:
        bits.append(b)
        b *= 2
    return tuple(bits)


def hooks_at(t, plan):
    for at, steps in plan.items():

        @pl.when(t == at)
        def _():
            for step in steps:
                step()


def layer_kernel(
    groups, row_blocks, bits, chunks,
    tok, cot, qkv_own, out_own, up_own, down_own, vec_own, lengths,
    mixed, o_down, o_up, o_out, o_qkv, o_tok, o_left, o_right, o_vec,
    out_w, up_w, down_w, ctxt, k_i, v_i, kt_i,
    w_v, x_v, q_v, ctx_v, lse, seg, vec_all, xhat, inv, g_hid, gx_side, vec_acc, vin, vacc, *scratch,
):
    r, h = place()
    own, width = tok.shape
    nb = own // BLK
    nw = nb + 2 * HALO
    halo = HALO * BLK
    shards = groups
    all_pairs = q_v.shape[0]
    pairs = all_pairs // 2
    half = pairs * 128
    shard_rows = half // 2
    x_half = (h // 2) % 2
    far_half = 1 - x_half
    core = h % 2
    rows = lambda b: pl.ds(pl.multiple_of(b * BLK, BLK), BLK)
    mean = lambda v: jnp.mean(v, axis=1, keepdims=True)
    n_chunks = len(chunks)
    (send, recv, keep, gsend, grecv, in_send, in_recv, side_send, side_recv, psend, precv, vsend, vrecv, loc) = scratch[6 * n_chunks :]
    sems = (send, recv, keep)
    turned = (1, 3, 6)
    outs = {"down": o_down, "up": o_up, "out": o_out, "q": o_qkv.at[0], "k": o_qkv.at[1], "v": o_qkv.at[2]}
    parts = [Sum(n, bits, scratch[6 * i : 6 * i + 6], sems, i, i in turned) for i, (_, _, n) in enumerate(chunks)]
    by_name = {}
    for part, (name, lo, _) in zip(parts, chunks):
        part.end = functools.partial(part.e, outs[name], lo)
        part.done = functools.partial(part.sent, outs[name], lo)
        by_name.setdefault(name, []).append(part)
    downs, ups, (out_c,) = by_name["down"], by_name["up"], by_name["out"]
    q_c, k_c, v_c = (by_name[name][0] for name in "qkv")
    one = parts[0]
    gq = Gather(qkv_own, w_v, (gsend, grecv), 0)
    go = Gather(out_own, out_w, (gsend, grecv), 1)
    gu = Gather(up_own, up_w, (gsend, grecv), 2)
    gd = Gather(down_own, down_w, (gsend, grecv), 3)

    def shard_of(i):
        across = 1 - i // 2
        other = 1 - i % 2
        return h + across * (2 - 4 * x_half) + other * (1 - 2 * core)

    def slot_of(i):
        return (i % 2) * (1 + i // 2)

    def fetch(src, dst, i):
        return pltpu.make_async_copy(src, dst, loc.at[i])

    vec_ids = [one.by_c, one.by_x, one.by_y, one.by_z] + one.by_rest

    def vstep(i):
        src = vec_acc if i == 0 else vacc.at[i - 1]
        return remote(src, vin.at[i], vsend.at[i], vrecv.at[i], vec_ids[i])

    def vnext(i):
        vstep(i).wait_recv()
        vacc[i] = (vec_acc[...] if i == 0 else vacc[i - 1]) + vin[i]
        if i + 1 < len(vec_ids):
            vstep(i + 1).start()

    def parameter(i):
        n = width // groups
        return jnp.concatenate([vec_all[s].astype(F32)[0:1, i * n : (i + 1) * n] for s in range(groups)], axis=1)

    def project(vt, k_s, v_s, kt_s, bias, ctx_t):
        total_blocks = groups * nb
        def to_right(i):
            src, dst = pl.ds(own - halo + i * BLK, BLK), pl.ds(i * BLK, BLK)
            return remote(tok.at[src, :], x_v.at[dst, :], in_send.at[i], in_recv.at[i], (r, h + 1))

        def to_left(i):
            src, dst = pl.ds(i * BLK, BLK), pl.ds(halo + own + i * BLK, BLK)
            return remote(tok.at[src, :], x_v.at[dst, :], in_send.at[HALO + i], in_recv.at[HALO + i], (r, h - 1))

        def both(to, step):
            for i in range(HALO):
                step(to(i))

        start, arrived, gone = (lambda c: c.start()), (lambda c: c.wait_recv()), (lambda c: c.wait_send())
        even = h % 2 == 0
        slow_right = jnp.logical_and(h % 2 == 1, h < groups - 1)
        slow_left = jnp.logical_and(even, h > 0)

        odd = h % 2 == 1

        def par(i):
            who = (r, lax.rem(h + 1 + i, groups))
            return remote(vec_own, vec_all.at[h], psend.at[i], precv.at[groups - 2 - i], who)

        def par_from(i):
            return remote(vec_own, vec_all.at[h], psend.at[i], precv.at[i], (r, lax.rem(h + 1 + i, groups)))

        mine = fetch(tok, x_v.at[pl.ds(halo, own), :], 0)
        mine.start()
        greet(group_of(r, h, groups) + [one.by_y, one.by_z] + one.by_rest)

        @pl.when(slow_right)
        def _():
            to_right(HALO - 1).start()

        @pl.when(slow_left)
        def _():
            to_left(0).start()

        @pl.when(even)
        def _():
            both(to_right, start)

        @pl.when(odd)
        def _():
            both(to_left, start)

        gq.start_c(True)
        gq.start_x()
        for i in range(groups - 1):
            par(i).start()
        vec_all[h] = vec_own[...]

        @pl.when(h == 0)
        def _():
            x_v[pl.ds(0, halo), :] = jnp.zeros((halo, width), BF)

        @pl.when(h == groups - 1)
        def _():
            x_v[pl.ds(halo + own, halo), :] = jnp.zeros((halo, width), BF)

        packed, docs = lengths.shape
        down = lax.broadcasted_iota(jnp.int32, (docs, docs), 0)
        across = lax.broadcasted_iota(jnp.int32, (docs, docs), 1)
        for b in range(nw):
            g = nb * h - HALO + b
            row = jnp.clip(g // row_blocks, 0, packed - 1)
            sizes = lengths[pl.ds(row, 1), :].astype(F32)
            ends = jnp.sum(jnp.where(across <= down, jnp.broadcast_to(sizes, (docs, docs)), 0.0), axis=1, keepdims=True)
            at = (lax.broadcasted_iota(jnp.int32, (docs, BLK), 1) + (g % row_blocks) * BLK).astype(F32)
            ids = jnp.sum(jnp.where(at >= ends, 1.0, 0.0), axis=0, keepdims=True) + (row * docs).astype(F32)
            inside = jnp.logical_and(g >= 0, g < total_blocks)
            seg[b] = jnp.where(inside, ids, -1.0)
        for j in range(nb):
            ws = window_start(h, j, nb, row_blocks)
            for kb in range(row_blocks):
                bias[j, kb] = mask_of(seg[ws + kb], seg[HALO + j])

        def project_keys(hx, b):
            base = pl.multiple_of(hx * half, 128)
            xb = x_v[rows(b), :]
            wk = w_v[1, pl.ds(base, half), :]
            wv = w_v[2, pl.ds(base, half), :]
            key = nt(xb, wk).astype(BF)
            value = nt(xb, wv).astype(BF)
            for i in range(pairs):
                k_s[hx * pairs + i, rows(b), :] = key[:, i * 128 : (i + 1) * 128]
                v_s[hx * pairs + i, rows(b), :] = value[:, i * 128 : (i + 1) * 128]
            kt_s[b, pl.ds(base, half), :] = nt(wk, xb).astype(BF)
            vt[b, pl.ds(base, half), :] = nt(wv, xb).astype(BF)

        def project_query(hx, b):
            base = pl.multiple_of(hx * half, 128)
            xb = x_v[rows(b + HALO), :]
            query = nt(xb, w_v[0, pl.ds(base, half), :]).astype(BF) * BF(HEAD_WIDTH**-0.5)
            for i in range(pairs):
                q_v[hx * pairs + i, rows(b), :] = query[:, i * 128 : (i + 1) * 128]

        def side_keys(hx, first):
            def body(b, c):
                project_keys(hx, first + b)
                return c

            lax.fori_loop(0, HALO, body, 0)

        def attend(hx, t):
            j = jnp.where(odd, t // pairs, nb - 1 - t // pairs)
            p = hx * pairs + t % pairs
            ws = window_start(h, j, nb, row_blocks)
            q = q_v[p, rows(j), :]
            lane = lax.broadcasted_iota(jnp.int32, q.shape, 1)
            q_both = jnp.concatenate([jnp.where(lane // HEAD_WIDTH == hh, q, jnp.zeros_like(q)) for hh in range(2)], axis=0)
            scores, tops = [[], []], [None, None]
            for kb in range(row_blocks):
                both_s = nt(k_s[p, rows(ws + kb), :], q_both)
                for hh in range(2):
                    s = both_s[:, hh * BLK : (hh + 1) * BLK] + bias[j, kb]
                    m = jnp.max(s.reshape(BLK // 8, 8, BLK), axis=0)
                    tops[hh] = m if kb == 0 else jnp.maximum(tops[hh], m)
                    scores[hh].append(s)
            tops = [jnp.max(m, axis=0, keepdims=True) for m in tops]
            totals = [jnp.zeros((8, BLK), F32) for _ in range(2)]
            accs = [jnp.zeros((HEAD_WIDTH, BLK), F32) for _ in range(2)]
            at = [pl.ds(pl.multiple_of((2 * p + hh) * HEAD_WIDTH, HEAD_WIDTH), HEAD_WIDTH) for hh in range(2)]
            for kb in range(row_blocks):
                for hh in range(2):
                    e = jnp.exp(scores[hh][kb] - tops[hh])
                    totals[hh] = totals[hh] + jnp.sum(e.reshape(BLK // 8, 8, BLK), axis=0)
                    accs[hh] = accs[hh] + nn(vt[ws + kb, at[hh], :], e.astype(BF))
            for hh in range(2):
                total = jnp.sum(totals[hh], axis=0, keepdims=True)
                ctx_t[j, at[hh], :] = accs[hh] / total
                lse[j, 2 * p + hh] = tops[hh] + jnp.log(total)

        def attend_all(hx, plan):
            def body(t, c):
                hooks_at(t, plan)
                attend(hx, t)
                return c

            lax.fori_loop(0, nb * pairs, body, 0)

        def slow_block(near):
            @pl.when(slow_right)
            def _():
                to_left(0 if near else 1).wait_recv()

            @pl.when(slow_left)
            def _():
                to_right(1 if near else 0).wait_recv()

            project_keys(x_half, jnp.where(odd, HALO + nb + (0 if near else 1), 1 if near else 0))

        def more_halo():
            @pl.when(slow_right)
            def _():
                to_right(0).start()

            @pl.when(slow_left)
            def _():
                to_left(1).start()

        mine.wait()
        gq.near(True)
        lax.fori_loop(0, nb, lambda b, c: (project_query(x_half, b), c)[1], 0)
        lax.fori_loop(HALO, HALO + nb, lambda b, c: (project_keys(x_half, b), c)[1], 0)

        @pl.when(odd)
        def _():
            both(to_right, arrived)

        @pl.when(even)
        def _():
            both(to_left, arrived)

        side_keys(x_half, jnp.where(odd, 0, HALO + nb))
        last = jnp.where(odd, nw - 1, 0)
        for i in range(all_pairs):
            k_s[i, rows(last), :] = jnp.zeros((BLK, 128), BF)
        vt[last] = jnp.zeros((width, BLK), BF)
        attend_all(x_half, {
            0: [lambda: go.start_c(True), lambda: gu.start_c(False)],
            2: [more_halo], 3: [gq.step_x, functools.partial(slow_block, True), lambda: gd.start_c(False)],
            6: [functools.partial(slow_block, False), go.start_x, gu.start_x], 7: [gq.step_yz],
        })
        gd.start_x()
        gq.step_diag()
        go.step_x()
        gq.far()
        lax.fori_loop(0, nb, lambda b, c: (project_query(far_half, b), c)[1], 0)
        lax.fori_loop(0, nw, lambda b, c: (project_keys(far_half, b), c)[1], 0)
        keys_out = [fetch(a, b, i) for i, (a, b) in enumerate(((k_s, k_i), (v_s, v_i), (kt_s, kt_i)))]
        for c in keys_out:
            c.start()
        attend_all(far_half, {
            0: [gu.step_x], 3: [go.step_yz], 7: [go.step_diag], 8: [gd.step_x, gu.step_yz],
        })
        ctx_out = fetch(ctx_t, ctxt, 3)
        ctx_out.start()
        for j in range(nb):
            ctx_v[j * BLK : (j + 1) * BLK, :] = ctx_t[j].T.astype(BF)
        go.near(True)
        go.far()
        for c in keys_out:
            c.wait()
        ctx_out.wait()
        for i in range(groups - 1):
            par(i).wait_send()
            par_from(i).wait_recv()

        @pl.when(h < groups - 1)
        def _():
            both(to_right, gone)

        @pl.when(h > 0)
        def _():
            both(to_left, gone)

    def dense(cot_v, out_v, up_v, down_v, hl, ht, act_t, slope):
        ffn, gup, mix_v, g_low = g_hid, hl, ctx_v, cot_v
        gain1, shift1, gain2, shift2 = (parameter(i) for i in range(4))
        first = [fetch(a, b, i) for i, (a, b) in enumerate(((out_w.at[0], out_v), (cot, cot_v)))]
        for c in first:
            c.start()

        def weights(i, slot):
            if i == shards - 1:
                return fetch(up_own.at[0], up_v.at[slot], 4 + slot), fetch(down_own.at[0], down_v.at[slot], 6 + slot)
            here = pl.ds(pl.multiple_of(shard_of(i) * width, 16), width)
            return fetch(up_w.at[0, here, :], up_v.at[slot], 4 + slot), fetch(down_w.at[0, here, :], down_v.at[slot], 6 + slot)

        def start_weights(i, slot):
            for c in weights(i, slot):
                c.start()

        def wait_weights(i, slot):
            for c in weights(i, slot):
                c.wait()

        start_weights(3, 0)
        gu.near(False)
        gd.near(False)
        start_weights(2, 1)
        vec_acc[...] = jnp.zeros_like(vec_acc)
        for c in first:
            c.wait()

        def before(b, c):
            resid = x_v[rows(b + HALO), :].astype(F32) + nn(ctx_v[rows(b), :], out_v[...])
            cen = resid - mean(resid)
            rs = lax.rsqrt(mean(cen * cen) + NORM_EPS)
            n = cen * rs
            hidden = n * gain1 + shift1
            xhat[rows(b), :] = n
            inv[rows(b), :] = jnp.broadcast_to(rs, (BLK, 128))
            low = hidden.astype(BF)
            hl[rows(b), :] = low
            ht[b] = low.T
            ffn[rows(b), :] = hidden
            return c

        lax.fori_loop(0, nb, before, 0)

        def forward(i, c):
            slot = i % 2
            wait_weights(0, slot)
            for b in range(nb):
                up = nn(hl[rows(b), :], up_v[slot])
                active, deriv = gelu_parts(up)
                active = active.astype(BF)
                slope[i, rows(b), :] = deriv.astype(BF)
                act_t[i, b] = active.T
                ffn[rows(b), :] += nn(active, down_v[slot])
            return c

        def forward_then(i, c):
            forward(i, c)
            hooks_at(i, {
                0: [gu.step_diag, gd.step_yz],
                1: [gd.step_diag, lambda: start_weights(1, 0)],
                2: [gu.far, gd.far, lambda: start_weights(0, 1)],
            })
            return c

        lax.fori_loop(0, shards, forward_then, 0)

        def middle(b, c):
            v = ffn[rows(b), :]
            cen = v - mean(v)
            rs = lax.rsqrt(mean(cen * cen) + NORM_EPS)
            n = cen * rs
            mix_v[rows(b), :] = (n * gain2 + shift2).astype(BF)
            ct = cot_v[rows(b), :].astype(F32)
            vec_acc[2:3, :] += jnp.sum(ct * n, axis=0, keepdims=True)
            vec_acc[3:4, :] += jnp.sum(ct, axis=0, keepdims=True)
            e = ct * gain2
            g = rs * (e - mean(e) - n * mean(e * n))
            g_hid[rows(b), :] = g
            g_low[rows(b), :] = g.astype(BF)
            return c

        lax.fori_loop(0, nb, middle, 0)
        mix_out = fetch(mix_v, mixed, 0)
        mix_out.start()

        def grad_rows(left, right, part, part_i, slot):
            n = part.n
            acc = jnp.zeros((n, width), F32)
            for b in range(nb):
                acc += nn(left(b, pl.ds(part_i * n, n)), right[b * BLK : (b + 1) * BLK, :])
            part.mine[slot] = acc.astype(BF)

        def down_grads(i, c):
            slot = slot_of(i)

            @pl.when(i == 2)
            def _():
                for p in downs:
                    p.core(0).wait_send()

            for k, p in enumerate(downs):
                grad_rows(lambda b, n: act_t[shards - 1 - i, b, n, :], g_low, p, k, slot)
            hooks_at(i, {
                0: [p.c0 for p in downs],
                1: [downs[0].f, downs[0].xs],
                2: [downs[1].f, *(p.c1 for p in downs)],
            })
            return c

        lax.fori_loop(0, shards, down_grads, 0)

        def backward(i, c):
            slot = 1 - i % 2

            @pl.when(i >= 2)
            def _():
                wait_weights(0, slot)

            def one_block(b, cc):
                ga = nt(g_low[rows(b), :], down_v[slot])
                gu = (slope[shards - 1 - i, rows(b), :].astype(F32) * ga).astype(BF)
                gup[rows(b), :] = gu
                g_hid[rows(b), :] += nt(gu, up_v[slot])
                return cc

            lax.fori_loop(0, nb, one_block, 0)

            for back in (0, 1):

                @pl.when(i == back)
                def _():
                    start_weights(back + 2, 1 - back)

            @pl.when(i == 2)
            def _():
                for p in ups:
                    p.core(0).wait_send()

            for k, p in enumerate(ups):
                grad_rows(lambda b, n: ht[b, n, :], gup, p, k, slot_of(i))
            hooks_at(i, {
                0: [p.c0 for p in ups] + [p.s for p in downs],
                1: [p.f for p in ups] + [downs[1].xs],
                2: [p.c1 for p in ups] + [downs[0].r],
                3: [p.s for p in ups],
            })
            return c

        lax.fori_loop(0, shards, backward, 0)
        mix_out.wait()

    pl.run_scoped(
        project,
        pltpu.VMEM((nw, width, BLK), BF),
        pltpu.VMEM((all_pairs, nw * BLK, 128), BF),
        pltpu.VMEM((all_pairs, nw * BLK, 128), BF),
        pltpu.VMEM((nw, width, BLK), BF),
        pltpu.VMEM((nb, row_blocks, BLK, BLK), F32),
        pltpu.VMEM((nb, width, BLK), F32),
    )
    pl.run_scoped(
        dense,
        pltpu.VMEM((own, width), BF),
        pltpu.VMEM((width, width), BF),
        pltpu.VMEM((2, width, width), BF),
        pltpu.VMEM((2, width, width), BF),
        pltpu.VMEM((own, width), BF),
        pltpu.VMEM((nb, width, BLK), BF),
        pltpu.VMEM((shards, nb, width, BLK), BF),
        pltpu.VMEM((shards, own, width), BF),
    )

    def attention(g_v, k_v, v_v, kt_v, delta, bias, dk, dv, dqt, dkt, dvt):
        gain1 = parameter(0)
        def keys(hf):
            base = pl.multiple_of(hf * half, 128)
            return (
                fetch(k_i.at[pl.ds(hf * pairs, pairs)], k_v, 0),
                fetch(v_i.at[pl.ds(hf * pairs, pairs)], v_v, 1),
                fetch(kt_i.at[:, pl.ds(base, half), :], kt_v, 2),
            )

        for c in keys(far_half):
            c.start()

        def between(out_v, ctxt_v):
            low_v = ctx_v
            o_in, c_in = fetch(out_w.at[0], out_v, 6), fetch(ctxt, ctxt_v, 7)
            o_in.start()
            c_in.start()

            def norm_back(b, c):
                g = g_hid[rows(b), :]
                n = xhat[rows(b), :]
                vec_acc[0:1, :] += jnp.sum(g * n, axis=0, keepdims=True)
                vec_acc[1:2, :] += jnp.sum(g, axis=0, keepdims=True)
                e = g * gain1
                res = inv[rows(b), 0:1] * (e - mean(e) - n * mean(e * n))
                g_hid[rows(b), :] = res
                low_v[rows(b), :] = res.astype(BF)
                return c

            lax.fori_loop(0, nb, norm_back, 0)
            o_in.wait()
            c_in.wait()

            def after(b, c):
                low = low_v[rows(b), :]
                gc = nt(low, out_v[...]).astype(BF)
                for i in range(all_pairs):
                    g_v[i, rows(b), :] = gc[:, i * 128 : (i + 1) * 128]
                prod = nt(out_v[...], low).astype(BF).astype(F32) * ctxt_v[b]
                for i in range(2 * all_pairs):
                    delta[b, i] = jnp.sum(prod[i * HEAD_WIDTH : (i + 1) * HEAD_WIDTH, :], axis=0, keepdims=True)
                return c

            lax.fori_loop(0, nb, after, 0)
            vstep(0).start()
            ups[0].xs()

            def grad_out(i, c):
                @pl.when(i == 2)
                def _():
                    out_c.core(0).wait_send()

                base = pl.multiple_of(shard_of(i) * shard_rows, 16)
                acc = jnp.zeros((shard_rows, width), F32)
                for b in range(nb):
                    acc += nn(ctxt_v[b, pl.ds(base, shard_rows), :].astype(BF), low_v[b * BLK : (b + 1) * BLK, :])
                out_c.mine[slot_of(i)] = acc.astype(BF)
                hooks_at(i, {0: [out_c.c0], 2: [out_c.c1]})
                return c

            lax.fori_loop(0, shards, grad_out, 0)
            downs[0].yy()
            downs[1].r()
            out_c.f()

        pl.run_scoped(
            between,
            pltpu.VMEM((width, width), BF),
            pltpu.VMEM((nb, width, BLK), F32),
        )
        def unit(hf, t):
            j, i = t // pairs, t % pairs
            p = hf * pairs + i
            ws = window_start(h, j, nb, row_blocks)

            @pl.when(i == 0)
            def _():
                for kb in range(row_blocks):
                    bias[kb * BLK : (kb + 1) * BLK, :] = mask_of(seg[ws + kb], seg[HALO + j])

            q = q_v[p, rows(j), :]
            g = g_v[p, rows(j), :]
            lane = lax.broadcasted_iota(jnp.int32, q.shape, 1)
            qm = [jnp.where(lane // HEAD_WIDTH == hh, q, jnp.zeros_like(q)) for hh in range(2)]
            gm = [jnp.where(lane // HEAD_WIDTH == hh, g, jnp.zeros_like(g)) for hh in range(2)]
            window = pl.ds(pl.multiple_of(ws * BLK, BLK), row_blocks * BLK)
            scores = nt(k_v[i, window, :], jnp.concatenate(qm, axis=0))
            g_probs = nt(v_v[i, window, :], jnp.concatenate(gm, axis=0))
            probs, g_scores = [], []
            for hh in range(2):
                cols = slice(hh * BLK, (hh + 1) * BLK)
                prob = jnp.exp(scores[:, cols] + bias[...] - lse[j, 2 * p + hh])
                g_scores.append((prob * (g_probs[:, cols] - delta[j, 2 * p + hh])).astype(BF))
                probs.append(prob.astype(BF))
            dv[i, window, :] += nn(probs[0], gm[0]) + nn(probs[1], gm[1])
            dk[i, window, :] += nn(g_scores[0], qm[0]) + nn(g_scores[1], qm[1])
            for hh in range(2):
                at = pl.ds(pl.multiple_of((2 * i + hh) * HEAD_WIDTH, HEAD_WIDTH), HEAD_WIDTH)
                acc = jnp.zeros((HEAD_WIDTH, BLK), F32)
                for kb in range(row_blocks):
                    acc += nn(kt_v[ws + kb, at, :], g_scores[hh][kb * BLK : (kb + 1) * BLK, :])
                dqt[j, at, :] = (acc * HEAD_WIDTH**-0.5).astype(BF)

        def attend_half(hf, plan, then):
            dk[...] = jnp.zeros_like(dk)
            dv[...] = jnp.zeros_like(dv)

            def body(t, c):
                hooks_at(t, plan)
                unit(hf, t)
                return c

            lax.fori_loop(0, nb * pairs, body, 0)
            for step in then:
                step()

            def turn(b, c):
                dkt[b] = jnp.concatenate([dk[p, rows(b), :].astype(BF) for p in range(pairs)], axis=1).T
                dvt[b] = jnp.concatenate([dv[p, rows(b), :].astype(BF) for p in range(pairs)], axis=1).T
                return c

            lax.fori_loop(0, nw, turn, 0)

        def weight_grads(which, slot, then):
            at = pl.multiple_of(which * shard_rows, 16)
            for c, src, blocks in ((q_c, dqt, range(HALO, HALO + nb)), (k_c, dkt, range(nw)), (v_c, dvt, range(nw))):
                acc = jnp.zeros((shard_rows, width), F32)
                for b in blocks:
                    acc += nn(src[b - blocks[0], pl.ds(at, shard_rows), :], x_v[b * BLK : (b + 1) * BLK, :])
                c.mine[slot] = acc.astype(BF)
                then(c)

        def input_grads(hf, last):
            base = pl.multiple_of(hf * half, 128)
            wk, wv = w_v.at[1, pl.ds(base, half), :], w_v.at[2, pl.ds(base, half), :]

            def block(b):
                kb = jnp.concatenate([dk[p, rows(b), :].astype(BF) for p in range(pairs)], axis=1)
                vb = jnp.concatenate([dv[p, rows(b), :].astype(BF) for p in range(pairs)], axis=1)
                return nn(kb, wk[...]) + nn(vb, wv[...])

            def side(i, c):
                b = i + jnp.where(i >= HALO, nb, 0)
                total = block(b)
                if last:
                    total = total + gx_side[rows(i), :].astype(F32)
                gx_side[rows(i), :] = total.astype(BF)
                return c

            lax.fori_loop(0, 2 * HALO, side, 0)

            def inner(j, c):
                g_hid[rows(j), :] += block(j + HALO) + nn(dqt[j].T, w_v[0, pl.ds(base, half), :])
                return c

            return lambda: lax.fori_loop(0, nb, inner, 0)

        for c in keys(far_half):
            c.wait()
        d0, d1 = downs
        u0, u1 = ups
        vs = [functools.partial(vnext, i) for i in range(len(vec_ids))]
        vs = [functools.partial(vnext, i) for i in range(len(vec_ids))]
        attend_half(far_half, {
            1: [vs[0], out_c.s], 3: [d0.zz], 5: [u1.xs], 6: [d1.yy], 7: [u0.r], 8: [d0.w],
        }, [d1.zz])
        for c in keys(x_half):
            c.start()
        weight_grads(1 - core, 0, lambda p: p.c0())
        out_c.xs()
        weight_grads(core, 1, lambda p: (p.f(), p.xs()))
        u0.yy()
        d0.u()
        input_grads(far_half, False)()
        u1.r()
        for c in keys(x_half):
            c.wait()
        attend_half(x_half, {
            1: [u0.zz, d1.w], 3: [out_c.r, vs[1]], 5: [u1.yy], 6: [u0.w], 7: [d0.end, d1.u], 8: [u1.zz, out_c.yy],
        }, [])
        for p in (q_c, k_c, v_c):
            p.core(0).wait_send()
        weight_grads(1 - core, 0, lambda p: p.c1())
        u0.u()
        out_c.zz()
        vs[2]()
        weight_grads(core, 2, lambda p: None)
        for p in (q_c, k_c, v_c):
            p.s()
            p.r()
        u1.w()
        finish = input_grads(x_half, True)

        @pl.when(h > 0)
        def _():
            to_left.start()

        @pl.when(h < groups - 1)
        def _():
            to_right.start()

        finish()
        q_c.yy()
        k_c.yy()
        out_c.w()
        q_c.zz()
        v_c.yy()
        k_c.zz()
        u1.u()
        v_c.zz()
        q_c.w()
        vs[3]()
        out_c.u()
        k_c.w()
        v_c.w()
        q_c.u()
        from_right, from_left = pl.ds(halo + own, halo), pl.ds(0, halo)

        @pl.when(h < groups - 1)
        def _():
            to_left.wait_recv()
            fetch(o_left, x_v.at[from_right, :], 0).start()

        @pl.when(h > 0)
        def _():
            to_right.wait_recv()
            fetch(o_right, x_v.at[from_left, :], 1).start()

        k_c.u()
        v_c.u()
        d1.end()
        u0.end()
        u1.end()
        out_c.end()
        for step in vs[4:]:
            step()

        @pl.when(h < groups - 1)
        def _():
            fetch(o_left, x_v.at[from_right, :], 0).wait()
            g_hid[own - halo :, :] += x_v[from_right, :].astype(F32)

        @pl.when(h > 0)
        def _():
            fetch(o_right, x_v.at[from_left, :], 1).wait()
            g_hid[:halo, :] += x_v[from_left, :].astype(F32)

        tok_out = fetch(g_hid, o_tok, 3)
        tok_out.start()
        for p in (q_c, k_c, v_c):
            p.end()
        tok_out.wait()

    to_left = remote(gx_side.at[pl.ds(0, halo), :], o_left, side_send.at[0], side_recv.at[0], (r, h - 1))
    to_right = remote(gx_side.at[pl.ds(halo, halo), :], o_right, side_send.at[1], side_recv.at[1], (r, h + 1))

    pl.run_scoped(
        attention,
        pltpu.VMEM((all_pairs, own, 128), BF),
        pltpu.VMEM((pairs, nw * BLK, 128), BF),
        pltpu.VMEM((pairs, nw * BLK, 128), BF),
        pltpu.VMEM((nw, half, BLK), BF),
        pltpu.VMEM((nb, 2 * all_pairs, 1, BLK), F32),
        pltpu.VMEM((row_blocks * BLK, BLK), F32),
        pltpu.VMEM((pairs, nw * BLK, 128), F32),
        pltpu.VMEM((pairs, nw * BLK, 128), F32),
        pltpu.VMEM((nb, half, BLK), BF),
        pltpu.VMEM((nw, half, BLK), BF),
        pltpu.VMEM((nw, half, BLK), BF),
    )

    o_vec[...] = vacc[len(vec_ids) - 1]
    for g in (gq, go, gu, gd):
        g.sent()
    for p in parts:
        p.done()
    for i in range(len(vec_ids)):
        vstep(i).wait_send()

    @pl.when(h > 0)
    def _():
        to_left.wait_send()

    @pl.when(h < groups - 1)
    def _():
        to_right.wait_send()


def layer(groups, row_blocks, row_devices, tok, cot, qkv_own, out_own, up_own, down_own, vec_own, lengths):
    own, width = tok.shape
    shard_rows = width // groups
    nb = own // BLK
    nw = nb + 2 * HALO
    all_pairs = width // 128
    bits = other_bits(row_devices)
    split = width // 2
    chunks = [(name, lo, split) for name in ("down", "up") for lo in range(0, width, split)]
    chunks += [(name, 0, shard_rows) for name in ("out", "q", "k", "v")]
    hops = 4 + len(bits)
    scratch = [
        pltpu.VMEM((3, width, width), BF),
        pltpu.VMEM((nw * BLK, width), BF),
        pltpu.VMEM((all_pairs, own, 128), BF),
        pltpu.VMEM((own, width), BF),
        pltpu.VMEM((nb, 2 * all_pairs, 1, BLK), F32),
        pltpu.VMEM((nw, 1, BLK), F32),
        pltpu.VMEM((groups,) + vec_own.shape, BF),
        pltpu.VMEM((own, width), F32),
        pltpu.VMEM((own, 128), F32),
        pltpu.VMEM((own, width), F32),
        pltpu.VMEM((2 * HALO * BLK, width), BF),
        pltpu.VMEM((8, width), F32),
        pltpu.VMEM((hops, 8, width), F32),
        pltpu.VMEM((hops, 8, width), F32),
    ]
    for _, _, n in chunks:
        scratch += [
            pltpu.VMEM((3, n, width), BF),
            pltpu.VMEM((2, n, width), BF),
            pltpu.VMEM((n, width), BF),
            pltpu.VMEM((n // 2, width), BF),
            pltpu.VMEM((n // 4, width), BF),
            pltpu.VMEM((max(1, len(bits)), n // 4, width), BF),
        ]
    dma = pltpu.SemaphoreType.DMA
    scratch += [dma((len(chunks), 8 + len(bits)))] * 2 + [dma((len(chunks), 3))] + [dma((4, 12))] * 2
    scratch += [dma((2 * HALO,))] * 2 + [dma((2,))] * 2 + [dma((groups - 1,))] * 2 + [dma((hops,))] * 2 + [dma((8,))]
    s = jax.ShapeDtypeStruct
    side = s((HALO * BLK, width), BF)
    outs = [
        (s((own, width), BF), ANY),
        (s((width, width), BF), ANY),
        (s((width, width), BF), ANY),
        (s((shard_rows, width), BF), ANY),
        (s((3, shard_rows, width), BF), ANY),
        (s((own, width), F32), ANY),
        (side, ANY),
        (side, ANY),
        (s((8, width), F32), VM),
        (s((1, width, width), BF), ANY),
        (s((1, groups * width, width), BF), ANY),
        (s((1, groups * width, width), BF), ANY),
        (s((nb, width, BLK), F32), ANY),
        (s((all_pairs, nw * BLK, 128), BF), ANY),
        (s((all_pairs, nw * BLK, 128), BF), ANY),
        (s((nw, width, BLK), BF), ANY),
    ]
    return pl.pallas_call(
        functools.partial(layer_kernel, groups, row_blocks, bits, chunks),
        out_shape=[o[0] for o in outs],
        in_specs=[ANY] * 6 + [VM] * 2,
        out_specs=[o[1] for o in outs],
        scratch_shapes=scratch,
        compiler_params=pltpu.CompilerParams(collective_id=0, has_side_effects=True, vmem_limit_bytes=VMEM_LIMIT),
        name="layer",
    )(tok, cot, qkv_own, out_own, up_own, down_own, vec_own, lengths)


def local(
    groups, row_devices,
    tokens, lengths, w_query, w_key, w_value, w_out, w_up, w_down,
    gain_first, shift_first, gain_second, shift_second, cotangent,
):
    packed_rows = lengths.shape[0]
    own, width = tokens.shape
    row_length = groups * own // packed_rows
    row_blocks = row_length // BLK
    h = lax.axis_index("heads")
    n_vec = gain_first.shape[0]
    vec_own = jnp.concatenate([gain_first, shift_first, gain_second, shift_second])
    vec_own = jnp.broadcast_to(vec_own[None, :], (16, width))
    qkv_own = jnp.stack([w_query.T, w_key.T, w_value.T])
    mixed, o_down, o_up, o_out, o_qkv, o_tok, _, _, o_vec = layer(
        groups, row_blocks, row_devices, tokens, cotangent, qkv_own, w_out[None], w_up[None], w_down[None], vec_own, lengths
    )[:9]
    mine = lax.dynamic_slice(o_vec, (0, n_vec * h), (4, n_vec))
    wide = lambda a: a.astype(F32)
    return (
        mixed, o_tok, wide(o_qkv[0].T), wide(o_qkv[1].T), wide(o_qkv[2].T), wide(o_out), wide(o_up), wide(o_down),
        mine[0], mine[1], mine[2], mine[3],
    )


def solution(mesh):
    both, heads = P(("rows", "heads"), None), P("heads")
    cols, rows = P(None, "heads"), P("heads", None)
    return jax.shard_map(
        functools.partial(local, mesh.shape["heads"], mesh.shape["rows"]),
        mesh=mesh,
        in_specs=(both, P("rows", None), cols, cols, cols, rows, cols, rows, heads, heads, heads, heads, both),
        out_specs=(both, both, cols, cols, cols, rows, cols, rows, heads, heads, heads, heads),
        check_vma=False,
    )
```

profile of v0, /device:TPU:0, one launch (start us, length us, event | category | flops | bytes accessed | tf_op | source)
XLA Modules:
  0.0 214.3 jit_solution(3725787314072618893)
XLA Ops:
  0.6 2.1 %pad_maximum_fusion.qkv_own = bf16[3,192,768]{2,1,0:T(8,128)(2,1)} fusion(bf16[1,192,768]{2,1,0:T(8,128)(2,1)} %bitcast.33, bf16[1,192,768]{2,1,0:T(8,128)(2,1)} %bitcast.34, bf16[1,192,768]{2,1,0:T(8,128)(2,1)} %bitcast.35), kind=kLoop, calls=%fused_computation | loop fusion | flops 884736 | bytes 1769472 | tf_op jit(solution)/shard_map/stack | solution.py:1176
  2.8 0.8 pad_maximum_fusion.1
  3.6 0.6 broadcast_in_dim.18.vec_own
  4.2 199.5 %layer.1 = (bf16[768,768]{1,0:T(8,128)(2,1)}, bf16[768,768]{1,0:T(8,128)(2,1)}, bf16[768,768]{1,0:T(8,128)(2,1)}, bf16[192,768]{1,0:T(8,128)(2,1)}, bf16[3,192,7...) custom-call(bf16[768,768]{1,0:T(8,128)(2,1)} %tok.1, ...), custom_call_target="tpu_custom_call" | custom-call | tf_op jit(solution)/shard_map/layer/pallas_call | solution.py:1152
  203.7 0.0 copy-start.2
  203.7 1.5 fusion
  205.2 2.4 %convert_bitcast_fusion = (f32[768,192]{0,1:T(8,128)}, f32[768,192]{0,1:T(8,128)}, f32[768,192]{0,1:T(8,128)}) fusion(bf16[3,192,768]{2,1,0:T(8,128)(2,1)} %get-tuple-element.21), kind=kLoop, calls=%fused_computation.1 | loop fusion | flops 442368 | bytes 2654208 | tf_op jit(solution)/shard_map/convert_element_type | solution.py:1181
  207.6 0.0 copy-start.1
  207.6 0.0 copy-done.2
  207.6 1.6 convert_element_type.46
  209.2 0.0 copy-start.4
  209.2 0.0 copy-start.3
  209.2 0.1 copy-done.1
  209.3 1.6 convert_element_type.47
  210.9 0.0 copy-start
  210.9 0.0 copy-done.4
  210.9 0.9 convert_element_type.45
  211.7 0.0 copy-done.3
  211.7 1.0 copy.27
  212.8 0.1 copy-done
  212.9 1.4 copy.28
Async XLA Ops:
  203.7 3.9 %copy-start.2 = (bf16[768,768]{1,0:T(8,128)(2,1)S(1)}, bf16[768,768]{1,0:T(8,128)(2,1)}, u32[]{:S(2)}) copy-start(bf16[768,768]{1,0:T(8,128)(2,1)} %get-tuple-element.23) | copy-start | bytes 3538948
  207.6 1.7 copy-start.1
  209.2 1.7 copy-start.4
  209.2 2.5 %copy-start.3 = (bf16[768,768]{1,0:T(8,128)(2,1)S(1)}, bf16[768,768]{1,0:T(8,128)(2,1)}, u32[]{:S(2)}) copy-start(bf16[768,768]{1,0:T(8,128)(2,1)} %get-tuple-element.45) | copy-start | bytes 3538948
  210.9 2.0 copy-start
where the time goes:
time: 215 us; the launch traced here: 214 us
  Pallas kernels  200 us (93%)
  other arithmetic  9.32 us (4%)
  local copies, waits for them, and re-layouts  4.78 us (2%)
    pallas_call x1, Pallas kernels, layer(): pl.pallas_call(functools.partial(layer_kernel, groups, row_blocks, bits,...  200 us
    convert_element_type x4, other arithmetic, local(): wide = lambda a: a.astype(F32)  6.39 us

commit v1 on v0

--- a/solution.py
+++ b/solution.py
@@ -448,16 +448,17 @@
         def _():
             to_left(0).start()
 
-        @pl.when(even)
-        def _():
-            both(to_right, start)
-
-        @pl.when(odd)
-        def _():
-            both(to_left, start)
-
         gq.start_c(True)
         gq.start_x()
+
+        @pl.when(even)
+        def _():
+            both(to_right, start)
+
+        @pl.when(odd)
+        def _():
+            both(to_left, start)
+
         for i in range(groups - 1):
             par(i).start()
         vec_all[h] = vec_own[...]
@@ -604,7 +605,7 @@
         for c in keys_out:
             c.start()
         attend_all(far_half, {
-            0: [gu.step_x], 3: [go.step_yz], 7: [go.step_diag], 8: [gd.step_x, gu.step_yz],
+            0: [gu.step_x], 3: [go.step_yz], 8: [gd.step_x, gu.step_yz, go.step_diag],
         })
         ctx_out = fetch(ctx_t, ctxt, 3)
         ctx_out.start()

time: 215 us -> 213 us (level)
  no operation moved by 1% of the time
where the time goes in v1:
time: 213 us
  Pallas kernels  198 us (93%)
  other arithmetic  9.32 us (4%)
  local copies, waits for them, and re-layouts  4.78 us (2%)
    pallas_call x1, Pallas kernels, layer(): pl.pallas_call(functools.partial(layer_kernel, groups, row_blocks, bits,...  198 us
    convert_element_type x4, other arithmetic, local(): wide = lambda a: a.astype(F32)  6.39 us

profile of v1, /device:TPU:0, one launch (start us, length us, event | category | flops | bytes accessed | tf_op | source)
XLA Modules:
  0.0 212.7 jit_solution(749917663851326786)
XLA Ops:
  0.6 2.1 %pad_maximum_fusion.qkv_own = bf16[3,192,768]{2,1,0:T(8,128)(2,1)} fusion(bf16[1,192,768]{2,1,0:T(8,128)(2,1)} %bitcast.33, bf16[1,192,768]{2,1,0:T(8,128)(2,1)} %bitcast.34, bf16[1,192,768]{2,1,0:T(8,128)(2,1)} %bitcast.35), kind=kLoop, calls=%fused_computation | loop fusion | flops 884736 | bytes 1769472 | tf_op jit(solution)/shard_map/stack | solution.py:1177
  2.8 0.8 pad_maximum_fusion.1
  3.6 0.6 broadcast_in_dim.18.vec_own
  4.2 197.9 %layer.1 = (bf16[768,768]{1,0:T(8,128)(2,1)}, bf16[768,768]{1,0:T(8,128)(2,1)}, bf16[768,768]{1,0:T(8,128)(2,1)}, bf16[192,768]{1,0:T(8,128)(2,1)}, bf16[3,192,7...) custom-call(bf16[768,768]{1,0:T(8,128)(2,1)} %tok.1, ...), custom_call_target="tpu_custom_call" | custom-call | tf_op jit(solution)/shard_map/layer/pallas_call | solution.py:1153
  202.1 0.0 copy-start.2
  202.2 1.5 fusion
  203.7 2.4 %convert_bitcast_fusion = (f32[768,192]{0,1:T(8,128)}, f32[768,192]{0,1:T(8,128)}, f32[768,192]{0,1:T(8,128)}) fusion(bf16[3,192,768]{2,1,0:T(8,128)(2,1)} %get-tuple-element.21), kind=kLoop, calls=%fused_computation.1 | loop fusion | flops 442368 | bytes 2654208 | tf_op jit(solution)/shard_map/convert_element_type | solution.py:1182
  206.1 0.0 copy-start.1
  206.1 0.0 copy-done.2
  206.1 1.6 convert_element_type.46
  207.6 0.0 copy-start.4
  207.6 0.0 copy-start.3
  207.6 0.1 copy-done.1
  207.7 1.6 convert_element_type.47
  209.3 0.0 copy-start
  209.3 0.0 copy-done.4
  209.3 0.9 convert_element_type.45
  210.2 0.0 copy-done.3
  210.2 1.0 copy.27
  211.2 0.1 copy-done
  211.3 1.4 copy.28
Async XLA Ops:
  202.1 3.9 %copy-start.2 = (bf16[768,768]{1,0:T(8,128)(2,1)S(1)}, bf16[768,768]{1,0:T(8,128)(2,1)}, u32[]{:S(2)}) copy-start(bf16[768,768]{1,0:T(8,128)(2,1)} %get-tuple-element.23) | copy-start | bytes 3538948
  206.1 1.7 copy-start.1
  207.6 1.7 copy-start.4
  207.6 2.5 %copy-start.3 = (bf16[768,768]{1,0:T(8,128)(2,1)S(1)}, bf16[768,768]{1,0:T(8,128)(2,1)}, u32[]{:S(2)}) copy-start(bf16[768,768]{1,0:T(8,128)(2,1)} %get-tuple-element.45) | copy-start | bytes 3538948
  209.3 2.0 copy-start
